TPU v7x, 32 devices: a whole 2x2x4 slice. The times are simulated.
32 devices in a mesh: grp: 2 (over x), exp: 16 (over z, y, core).
Axes of the slice: x: 2, y: 2, z: 4, core: 2. Of those that a mesh axis runs over, the one named last changes fastest.
Arguments:
- tokens: bfloat16 [512, 4096], P(('grp', 'exp')), parts along dimension 0, may hold values from -6 to 6
- norm_gain: float32 [4096], replicated, may hold values from 0.1 to 1.9
- gate_weight: bfloat16 [4096, 24576], P(None, 'exp'), may hold values from -0.09375 to 0.09375
- up_weight: bfloat16 [4096, 24576], P(None, 'exp'), may hold values from -0.09375 to 0.09375
- down_weight: bfloat16 [24576, 4096], P('exp'), may hold values from -0.15625 to 0.15625
- routes: int32 [512, 8], P(('grp', 'exp')), parts along dimension 0, may hold values from 0 to 15, all different within a row; in each aligned block of 16 rows (0 to 15, 16 to 31, ...) at most 9 rows name the same one
- fractions: int32 [512, 8], P(('grp', 'exp')), parts along dimension 0, may hold values from 1 to 16
- cotangent: bfloat16 [512, 4096], P(('grp', 'exp')), parts along dimension 0, may hold values from -6 to 6
Outputs:
- mixed: bfloat16 [512, 4096], P(('grp', 'exp')), parts along dimension 0
- token_grad: bfloat16 [512, 4096], P(('grp', 'exp')), parts along dimension 0
There are 2 independent parts, one for each index of `grp`. A program takes and returns all parts, laid end to end along the dimension named above; an argument that names none is the same for every part. Nothing has to cross between parts.
Inputs may be any that keep to these rules, and one draw needn't show every extreme that they name: `routes`: each row names 8 different experts. Among the 16 rows of one device, at most 9 name one expert, a bound that some block reaches of them.
All inputs are finite; a program needn't handle non-finite values.
Results may differ from a plain program's by a relative error of at most 0.0071.
Values may be sent and summed in bfloat16 or wider, within the bound.
A program may use at most 128 MiB of HBM per device.

v0:
```python
import jax
import jax.numpy as jnp
from jax import lax
from jax.sharding import PartitionSpec as P

EXPERTS = 16
CAP = 9


def normalize(values, gain):
    scale = lax.rsqrt(jnp.mean(values * values, axis=-1, keepdims=True) + 1e-06)
    return values * scale * gain


def local(tokens, norm_gain, gate_weight, up_weight, down_weight, routes, fractions, cotangent):
    group = lax.axis_size("exp") // EXPERTS
    width = tokens.shape[1]
    values = tokens.astype(jnp.float32)
    normed, pullback = jax.vjp(lambda v: normalize(v, norm_gain), values)
    normed_b = normed.astype(jnp.bfloat16)
    shares = fractions.astype(jnp.float32)
    shares = shares / jnp.sum(shares, axis=-1, keepdims=True)
    named = (routes[:, :, None] == jnp.arange(EXPERTS, dtype=jnp.int32)[None, None, :]).astype(
        jnp.int32
    )
    per_expert = jnp.sum(named, axis=1)
    before = jnp.cumsum(per_expert, axis=0) - per_expert
    slot_index = jnp.sum(named * before[:, None, :], axis=2)
    position = routes * CAP + slot_index
    placed = position[:, :, None] == jnp.arange(EXPERTS * CAP, dtype=jnp.int32)[None, None, :]
    dispatch_map = jnp.sum(placed.astype(jnp.float32), axis=1).astype(jnp.bfloat16)
    combine_map = jnp.sum(jnp.where(placed, shares[:, :, None], jnp.float32(0.0)), axis=1)

    def bucket(rows):
        filled = jnp.einsum("ts,td->sd", dispatch_map, rows, preferred_element_type=jnp.float32)
        filled = filled.astype(jnp.bfloat16).reshape(EXPERTS, 1, CAP, width)
        return jnp.broadcast_to(filled, (EXPERTS, group, CAP, width)).reshape(
            EXPERTS * group, CAP, width
        )

    rows_in = lax.all_to_all(bucket(normed_b), "exp", split_axis=0, concat_axis=0, tiled=True)
    grads_in = lax.all_to_all(bucket(cotangent), "exp", split_axis=0, concat_axis=0, tiled=True)
    shape = rows_in.shape
    rows = rows_in.reshape(-1, width)
    grads = grads_in.reshape(-1, width)
    gate = jnp.dot(rows, gate_weight, preferred_element_type=jnp.float32)
    upper = jnp.dot(rows, up_weight, preferred_element_type=jnp.float32)
    sigma = jax.nn.sigmoid(gate)
    silu_gate = gate * sigma
    act = (silu_gate * upper).astype(jnp.bfloat16)
    output = jnp.dot(act, down_weight, preferred_element_type=jnp.float32)
    dact = jnp.dot(grads, down_weight.T, preferred_element_type=jnp.float32)
    dgate = (dact * upper * sigma * (1.0 + gate * (1.0 - sigma))).astype(jnp.bfloat16)
    dup = (dact * silu_gate).astype(jnp.bfloat16)
    backed = jnp.dot(dgate, gate_weight.T, preferred_element_type=jnp.float32)
    backed = backed + jnp.dot(dup, up_weight.T, preferred_element_type=jnp.float32)
    terms = jnp.stack([output.reshape(shape), backed.reshape(shape)], axis=0)
    rounded_terms = terms.astype(jnp.bfloat16)
    arrived = lax.all_to_all(rounded_terms, "exp", split_axis=1, concat_axis=1, tiled=True)
    summed = jnp.sum(arrived.reshape(2, EXPERTS, group, CAP, width).astype(jnp.float32), axis=2)
    results = summed.astype(jnp.bfloat16).reshape(2, EXPERTS * CAP, width)
    mixed = jnp.dot(combine_map, results[0].astype(jnp.float32), precision=lax.Precision.HIGHEST)
    dnormed = jnp.dot(combine_map, results[1].astype(jnp.float32), precision=lax.Precision.HIGHEST)
    token_grad = pullback(dnormed)[0]
    return (mixed.astype(jnp.bfloat16), token_grad.astype(jnp.bfloat16))


def solution(mesh):
    placed = (
        P(("grp", "exp"), None),
        P(),
        P(None, "exp"),
        P(None, "exp"),
        P("exp", None),
        P(("grp", "exp"), None),
        P(("grp", "exp"), None),
        P(("grp", "exp"), None),
    )
    return jax.shard_map(
        local,
        mesh=mesh,
        in_specs=placed,
        out_specs=(P(("grp", "exp"), None), P(("grp", "exp"), None)),
        check_vma=False,
    )
```

profile of v0, /device:TPU:0, one launch (start us, length us, event | category | flops | bytes accessed | tf_op | source)
XLA Modules:
  0.0 239.2 jit_solution(5405765429618341010)
XLA Ops:
  4.7 1.4 convolution_convert_fusion.2
  6.2 1.6 reshape_reshape.6
  7.7 7.4 %all-to-all-start = ((bf16[16,9,4096]{2,1,0:T(8,128)(2,1)}), bf16[16,9,4096]{2,1,0:T(8,128)(2,1)S(1)}, u32[]{:S(2)}, u32[]{:S(2)}) async-start(bf16[16,9,4096]{2,1,0:T(8,128)(2,1)} %reshape_reshape.6), calls=%async_computation | async-start | bytes 4194304 | tf_op jit(solution)/shard_map/all_to_all | solution.py:41
  15.6 1.6 reshape_reshape.7
  17.2 39.0 %all-to-all-done = bf16[16,9,4096]{2,1,0:T(8,128)(2,1)S(1)} async-done(((bf16[16,9,4096]{2,1,0:T(8,128)(2,1)}), bf16[16,9,4096]{2,1,0:T(8,128)(2,1)S(1)}, u32[]{:S(2)}, u32[]{:S(2)}) %all-to-all-start) | async-done | bytes 1179680 | tf_op jit(solution)/shard_map/all_to_all | solution.py:41
  56.2 11.3 %all-to-all-start.1 = ((bf16[16,9,4096]{2,1,0:T(8,128)(2,1)}), bf16[16,9,4096]{2,1,0:T(8,128)(2,1)}, u32[]{:S(2)}, u32[]{:S(2)}) async-start(bf16[16,9,4096]{2,1,0:T(8,128)(2,1)} %reshape_reshape.7), calls=%async_computation.1 | async-start | bytes 4194304 | tf_op jit(solution)/shard_map/all_to_all | solution.py:42
  68.1 6.6 %fusion.20 = f32[144,1536]{1,0:T(8,128)S(1)} fusion(bf16[144,4096]{1,0:T(8,128)(2,1)S(1)} %reshape.49, bf16[4096,1536]{1,0:T(8,128)(2,1)} %param.10), kind=kOutput, calls=%fused_computation.46 | convolution fusion | flops 1811939328 | bytes 14647296 | tf_op jit(solution)/shard_map/dot_general | solution.py:46
  74.7 7.8 %fusion.21 = f32[144,1536]{1,0:T(8,128)} fusion(bf16[144,4096]{1,0:T(8,128)(2,1)S(1)} %reshape.49, bf16[4096,1536]{1,0:T(8,128)(2,1)} %param.11), kind=kOutput, calls=%fused_computation.47 | convolution fusion | flops 1811939328 | bytes 14647296 | tf_op jit(solution)/shard_map/dot_general | solution.py:47
  82.5 26.2 %all-to-all-done.1 = bf16[16,9,4096]{2,1,0:T(8,128)(2,1)} async-done(((bf16[16,9,4096]{2,1,0:T(8,128)(2,1)}), bf16[16,9,4096]{2,1,0:T(8,128)(2,1)}, u32[]{:S(2)}, u32[]{:S(2)}) %all-to-all-start.1) | async-done | bytes 1179680 | tf_op jit(solution)/shard_map/all_to_all | solution.py:42
  108.7 1.8 reshape.50
  110.5 8.9 %fusion.22 = f32[144,1536]{1,0:T(8,128)S(1)} fusion(bf16[144,4096]{1,0:T(8,128)(2,1)S(1)} %reshape.50, bf16[1536,4096]{1,0:T(8,128)(2,1)} %param.12), kind=kOutput, calls=%fused_computation.48 | convolution fusion | flops 1811939328 | bytes 14647296 | tf_op jit(solution)/shard_map/dot_general | solution.py:52
  119.4 7.7 %convolution_convert_fusion.1 = bf16[144,4096]{1,0:T(8,128)(2,1)} fusion(bf16[1536,4096]{1,0:T(8,128)(2,1)} %param.12, f32[144,1536]{1,0:T(8,128)S(1)} %copy-done.4, f32[144,1536]{1,0:T(8,128)S(1)} %fusion.20), kind=kOutput, calls=%fused_computation.3 | convolution fusion | flops 1813856256 | bytes 15532032 | tf_op jit(solution)/shard_map/dot_general | solution.py:51
  127.1 1.8 stack_reshape.8
  128.9 9.4 %fusion.2 = f32[144,4096]{1,0:T(8,128)S(1)} fusion(bf16[4096,1536]{1,0:T(8,128)(2,1)} %param.10, f32[144,1536]{1,0:T(8,128)} %copy-done.2, f32[144,1536]{1,0:T(8,128)S(1)} %fusion.22, f32[144,1536]{1,0:T(8,128)} %fusion.21), kind=kOutput, calls=%fused_computation.19 | convolution fusion | flops 1814151168 | bytes 17596416 | tf_op jit(solution)/shard_map/dot_general | solution.py:55
  138.3 9.9 %fusion = bf16[144,4096]{1,0:T(8,128)(2,1)} fusion(f32[144,4096]{1,0:T(8,128)S(1)} %fusion.2, bf16[4096,1536]{1,0:T(8,128)(2,1)} %param.11, f32[144,1536]{1,0:T(8,128)S(1)} %fusion.22, f32[144,1536]{1,0:T(8,128)S(1)} %copy-done.3), kind=kOutput, calls=%fused_computation.1 | convolution fusion | flops 1814446080 | bytes 17891328 | tf_op jit(solution)/shard_map/dot_general | solution.py:56
  148.2 2.7 %stack_reshape.9 = bf16[1,16,9,4096]{3,2,1,0:T(8,128)(2,1)} reshape(bf16[144,4096]{1,0:T(8,128)(2,1)} %fusion) | data formatting | bytes 2359296 | tf_op jit(solution)/shard_map/stack;reshape | solution.py:57
  150.8 2.1 pad_maximum_fusion
  152.9 2.6 %copy.23 = bf16[2,16,9,4096]{3,0,2,1:T(2,128)(2,1)S(1)} copy(bf16[2,16,9,4096]{3,2,1,0:T(8,128)(2,1)S(1)} %pad_maximum_fusion) | data formatting | bytes 4718592 | tf_op jit(solution)/shard_map/stack | solution.py:57
  155.6 65.0 %all_to_all.15 = bf16[2,16,9,4096]{3,0,2,1:T(2,128)(2,1)S(1)} all-to-all(bf16[2,16,9,4096]{3,0,2,1:T(2,128)(2,1)S(1)} %copy.23), channel_id=1, replica_groups=mesh['grp'=2,'exp'=16] {'exp'}, dimensions={1} | all-to-all | bytes 4718592 | tf_op jit(solution)/shard_map/all_to_all | solution.py:59
  220.6 11.3 %slice_reduce_fusion = (bf16[16,9,4096]{2,1,0:T(8,128)(2,1)}, bf16[16,9,4096]{2,1,0:T(8,128)(2,1)S(1)}) fusion(bf16[2,16,9,4096]{3,0,2,1:T(2,128)(2,1)S(1)} %all_to_all.15), kind=kLoop, calls=%fused_computation.8 | loop fusion | bytes 4718592 | tf_op jit(solution)/shard_map/slice | solution.py:63
  231.8 1.8 squeeze.7
  233.7 1.4 fusion.8
  236.2 1.2 convolution_convert_fusion.3
  237.5 1.7 fusion.4
  (36 shorter events, 6.3 us)
Async XLA Ops:
  0.6 14.5 %copy-start = (bf16[16,4096]{1,0:T(8,128)(2,1)S(1)}, bf16[16,4096]{1,0:T(8,128)(2,1)}, u32[]{:S(2)}) copy-start(bf16[16,4096]{1,0:T(8,128)(2,1)} %param.15) | copy-start | bytes 393220
  1.7 0.7 copy-start.8
  1.8 6.0 %copy-start.7 = (f32[16]{0:T(128)}, f32[16]{0:T(128)S(1)}, u32[]{:S(2)}) copy-start(f32[16]{0:T(128)S(1)} %fusion.16) | copy-start | bytes 196
  7.7 48.5 %all-to-all-start = ((bf16[16,9,4096]{2,1,0:T(8,128)(2,1)}), bf16[16,9,4096]{2,1,0:T(8,128)(2,1)S(1)}, u32[]{:S(2)}, u32[]{:S(2)}) async-start(bf16[16,9,4096]{2,1,0:T(8,128)(2,1)} %reshape_reshape.6), calls=%async_computation | async-start | bytes 4194304 | tf_op jit(solution)/shard_map/all_to_all | solution.py:41
  56.2 52.4 %all-to-all-start.1 = ((bf16[16,9,4096]{2,1,0:T(8,128)(2,1)}), bf16[16,9,4096]{2,1,0:T(8,128)(2,1)}, u32[]{:S(2)}, u32[]{:S(2)}) async-start(bf16[16,9,4096]{2,1,0:T(8,128)(2,1)} %reshape_reshape.7), calls=%async_computation.1 | async-start | bytes 4194304 | tf_op jit(solution)/shard_map/all_to_all | solution.py:42
  74.6 44.8 %copy-start.2 = (f32[144,1536]{1,0:T(8,128)}, f32[144,1536]{1,0:T(8,128)S(1)}, u32[]{:S(2)}) copy-start(f32[144,1536]{1,0:T(8,128)S(1)} %fusion.20) | copy-start | bytes 2654212
  110.5 9.0 %copy-start.4 = (f32[144,1536]{1,0:T(8,128)S(1)}, f32[144,1536]{1,0:T(8,128)}, u32[]{:S(2)}) copy-start(f32[144,1536]{1,0:T(8,128)} %fusion.21) | copy-start | bytes 2654212
  128.9 9.4 %copy-start.3 = (f32[144,1536]{1,0:T(8,128)S(1)}, f32[144,1536]{1,0:T(8,128)}, u32[]{:S(2)}) copy-start(f32[144,1536]{1,0:T(8,128)} %copy-done.2) | copy-start | bytes 2654212
  231.8 1.9 copy-start.5
  231.8 1.9 copy-start.6
  231.8 3.3 %copy-start.9 = (f32[16]{0:T(128)S(1)}, f32[16]{0:T(128)}, u32[]{:S(2)}) copy-start(f32[16]{0:T(128)} %copy-done.8) | copy-start | bytes 196
  235.7 3.5 %copy-start.1 = (bf16[16,4096]{1,0:T(8,128)(2,1)S(1)}, bf16[16,4096]{1,0:T(8,128)(2,1)}, u32[]{:S(2)}) copy-start(bf16[16,4096]{1,0:T(8,128)(2,1)} %param.15) | copy-start | bytes 393220
where the time goes:
time: 240 us; the launch traced here: 239 us
  waiting for transfers between devices  65.2 us (27%)
  blocking collectives  65 us (27%)
  matrix products  54.8 us (23%)
  local copies, waits for them, and re-layouts  27.1 us (11%)
  starting transfers between devices  18.7 us (8%)
  other arithmetic  7.64 us (3%)
    all_to_all x1, blocking collectives, local(): lax.all_to_all(rounded_terms, 'exp', split_axis=1, concat_axis=1, tiled=T...  65 us
    all_to_all x1, waiting for transfers between devices, local(): lax.all_to_all(bucket(normed_b), 'exp', split_axis=0, concat_axis=0, tile...  39 us
    all_to_all x1, waiting for transfers between devices, local(): lax.all_to_all(bucket(cotangent), 'exp', split_axis=0, concat_axis=0, til...  26.2 us
    all_to_all x1, starting transfers between devices, local(): lax.all_to_all(bucket(cotangent), 'exp', split_axis=0, concat_axis=0, til...  11.3 us
    slice x1, local copies, waits for them, and re-layouts, local(): results[1].astype(jnp.float32)  11.3 us
    dot_general x1, matrix products, local(): jnp.dot(dup, up_weight.T, preferred_element_type=jnp.float32)  9.87 us
    dot_general x1, matrix products, local(): backed = jnp.dot(dgate, gate_weight.T, preferred_element_type=jnp.float32)  9.39 us
    dot_general x1, matrix products, local(): dact = jnp.dot(grads, down_weight.T, preferred_element_type=jnp.float32)  8.94 us
  transfers between devices with their start and end apart: 2, of which 2 were waited for; matrix products, arithmetic and copies ran while one was open for 7% of the time, Pallas kernels for 0%

commit v1 on v0

v1 whole, which is shorter than its diff:
```python
import functools

import jax
import jax.numpy as jnp
from jax import lax
from jax.experimental import pallas as pl
from jax.experimental.pallas import tpu as pltpu
from jax.sharding import PartitionSpec as P

EXPERTS = 16
LANES = 128
LEAD = 2
MESH = pl.DeviceIdType.MESH
F32 = jnp.float32
BF16 = jnp.bfloat16


def dot(a, b):
    return lax.dot_general(a, b, (((1,), (0,)), ((), ())), preferred_element_type=F32)


def dot_t(a, b):
    return lax.dot_general(a, b, (((1,), (1,)), ((), ())), preferred_element_type=F32)


def kernel(
    nz,
    ny,
    chunks,
    tokens,
    gain,
    routes,
    fractions,
    cotangent,
    w_gate,
    w_up,
    w_down,
    mixed,
    token_grad,
    data,
    gate_v,
    up_v,
    down_v,
    gate,
    upper,
    dact,
    act,
    dgate,
    dup,
    from_core,
    from_y,
    from_z,
    final,
    w_sem,
    zs,
    zr,
    ys,
    yr,
    cs,
    cr,
    a_s,
    a_r,
    b_s,
    b_r,
    ps,
    pr,
):
    rows, width = tokens.shape
    cols = width // chunks
    hidden = w_gate.shape[1]
    total = 2 * ny * nz * rows
    me = lax.axis_index("exp")
    c = lax.rem(me, 2)
    y = lax.rem(me // 2, ny)
    z = me // (2 * ny)

    def at(zz, yy, cc):
        return (zz * ny + yy) * 2 + cc

    sibling = at(z, y, 1 - c)
    across = at(z, ny - 1 - y, c)
    ahead = at(z + 1, y, c)
    behind = at(z - 1, y, c)

    def weights(q):
        part = pl.ds(q * cols, cols)
        return (
            pltpu.make_async_copy(w_gate.at[part, :], gate_v.at[q], w_sem.at[q, 0]),
            pltpu.make_async_copy(w_up.at[part, :], up_v.at[q], w_sem.at[q, 1]),
            pltpu.make_async_copy(w_down.at[:, part], down_v.at[q], w_sem.at[q, 2]),
        )

    barrier = pltpu.get_barrier_semaphore()

    def greet(device):
        pl.semaphore_signal(barrier, inc=1, device_id={"exp": device}, device_id_type=MESH)

    greet(sibling)
    if ny > 1:
        greet(across)
    pl.when(z + 1 < nz)(lambda: greet(ahead))
    pl.when(z > 0)(lambda: greet(behind))

    for q in range(chunks):
        for copy in weights(q):
            copy.start()

    values = tokens[...].astype(F32)
    scale = lax.rsqrt(jnp.mean(values * values, axis=-1, keepdims=True) + 1e-06)
    normed = (values * scale * gain[...]).astype(BF16)
    own = pl.ds(pl.multiple_of(((c * ny + y) * nz + z) * rows, rows), rows)
    lane = lax.broadcasted_iota(jnp.int32, (rows, LANES), 1)
    table = jnp.zeros((rows, LANES), F32)
    for k in range(routes.shape[1]):
        table = table + jnp.where(
            routes[:, k : k + 1] == lane, fractions[:, k : k + 1].astype(F32), 0.0
        )
    data[0, own, 2 * cols :] = table.astype(BF16)
    for q in range(chunks):
        data[q, own, :cols] = normed[:, q * cols : (q + 1) * cols]
        data[q, own, cols : 2 * cols] = cotangent[:, q * cols : (q + 1) * cols]

    peers = jnp.int32(2 if ny > 1 else 1) + (z + 1 < nz).astype(jnp.int32) + (z > 0).astype(jnp.int32)
    pl.semaphore_wait(barrier, peers)

    def span(q):
        return 2 * cols + (LANES if q == 0 else 0)

    def place(cc, yy, zz):
        return pl.multiple_of(((cc * ny + yy) * nz + zz) * rows, rows)

    def held(q, cc, yy, zz, count=1, columns=None):
        return data.at[
            q, pl.ds(place(cc, yy, zz), count * rows), pl.ds(0, span(q) if columns is None else columns)
        ]

    def remote(src, dst, send, recv, device):
        return pltpu.make_async_remote_copy(
            src_ref=src,
            dst_ref=dst,
            send_sem=send,
            recv_sem=recv,
            device_id={"exp": device},
            device_id_type=MESH,
        )

    def z_copy(q, way, hop, block):
        ref = held(q, c, y, block)
        return remote(
            ref, ref, zs.at[q, way, hop - 1], zr.at[q, way, hop - 1], ahead if way == 0 else behind
        )

    def z_sends(q, hop, act_on):
        pl.when((z + 1 < nz) & (z >= hop - 1))(lambda: act_on(z_copy(q, 0, hop, z - hop + 1)))
        pl.when((z > 0) & (z + hop - 1 < nz))(lambda: act_on(z_copy(q, 1, hop, z + hop - 1)))

    def y_copy(q, block, yy):
        ref = held(q, c, yy, block)
        return remote(ref, ref, ys.at[q, block], yr.at[q, block], across)

    def c_copy(q, cc, half):
        ref = held(q, cc, y if half == 0 else ny - 1 - y, 0, nz)
        return remote(ref, ref, cs.at[q, half], cr.at[q, half], sibling)

    def begin(q):
        z_sends(q, 1, lambda copy: copy.start())
        if ny > 1:
            y_copy(q, z, y).start()

    def gather_hop(q, hop):
        def arrived(way, block):
            z_copy(q, way, hop, block).wait_recv()
            if ny > 1:
                y_copy(q, block, y).start()

        pl.when(z >= hop)(lambda: arrived(0, z - hop))
        pl.when(z + hop < nz)(lambda: arrived(1, z + hop))
        if hop < nz - 1:
            z_sends(q, hop + 1, lambda copy: copy.start())
        else:
            c_copy(q, c, 0).start()

    def gather_across(q):
        if ny > 1:
            for block in range(nz):
                y_copy(q, block, ny - 1 - y).wait_recv()
            c_copy(q, c, 1).start()

    step = 256 if total % 256 == 0 else total
    tile = 256 if hidden % 256 == 0 else LANES

    def first(q):
        c_copy(q, 1 - c, 0).wait_recv()
        if ny > 1:
            c_copy(q, 1 - c, 1).wait_recv()
        for copy in weights(q):
            copy.wait()
        for low in range(0, total, step):
            some = slice(low, low + step)

            @pl.loop(0, hidden // tile)
            def _(n):
                part = pl.ds(pl.multiple_of(n * tile, tile), tile)
                x = data[q, some, :cols]
                g = dot(x, gate_v[q, :, part])
                u = dot(x, up_v[q, :, part])
                d = dot_t(data[q, some, cols : 2 * cols], down_v[q, part, :])
                if q == 0:
                    gate[some, part] = g
                    upper[some, part] = u
                    dact[some, part] = d
                else:
                    gate[some, part] += g
                    upper[some, part] += u
                    dact[some, part] += d

    for q in range(min(LEAD, chunks)):
        begin(q)
    for slot in range(chunks + nz + 1):
        if LEAD <= slot + LEAD < chunks:
            begin(slot + LEAD)
        for stage in range(nz, 0, -1):
            q = slot - stage + 1
            if 0 <= q < chunks:
                if stage < nz:
                    gather_hop(q, stage)
                else:
                    gather_across(q)
        if 0 <= slot - nz < chunks:
            first(slot - nz)

    for q in range(chunks):
        for hop in range(1, nz):
            z_sends(q, hop, lambda copy: copy.wait_send())
        if ny > 1:
            for block in range(nz):
                y_copy(q, block, y).wait_send()
            c_copy(q, c, 1).wait_send()
        c_copy(q, c, 0).wait_send()

    mine = me // (2 * ny * nz // EXPERTS)
    for low in range(0, total, step):
        some = slice(low, low + step)
        named = data[0, some, 2 * cols :].astype(F32)
        lanes = lax.broadcasted_iota(jnp.int32, named.shape, 1)
        share = jnp.sum(jnp.where(lanes == mine, named, 0.0), axis=1, keepdims=True)
        share = share / jnp.sum(named, axis=1, keepdims=True)

        @pl.loop(0, hidden // LANES)
        def _(n):
            part = pl.ds(pl.multiple_of(n * LANES, LANES), LANES)
            g = gate[some, part]
            u = upper[some, part]
            d = dact[some, part] * share
            sigma = jax.nn.sigmoid(g)
            silu = g * sigma
            act[some, part] = (silu * u * share).astype(BF16)
            dgate[some, part] = (d * u * sigma * (1.0 + g * (1.0 - sigma))).astype(BF16)
            dup[some, part] = (d * silu).astype(BF16)

    def a_copy(q):
        return remote(
            held(q, 1 - c, 0, 0, ny * nz, 2 * cols), from_core.at[q], a_s.at[q], a_r.at[q], sibling
        )

    def b_copy(q):
        return remote(
            held(q, c, ny - 1 - y, 0, nz, 2 * cols), from_y.at[q], b_s.at[q], b_r.at[q], across
        )

    def landing(q, way, block):
        return from_z.at[q, pl.ds(pl.multiple_of((block + 1 - way) * rows, rows), rows), :]

    def p_copy(q, way, hop, block):
        return remote(
            held(q, c, y, block, 1, 2 * cols),
            landing(q, way, block),
            ps.at[q, way, hop - 1],
            pr.at[q, way, hop - 1],
            ahead if way == 0 else behind,
        )

    def p_sends(q, hop, act_on):
        pl.when(z < hop)(lambda: act_on(p_copy(q, 0, hop, z + nz - hop)))
        pl.when(nz - 1 - z < hop)(lambda: act_on(p_copy(q, 1, hop, z - nz + hop)))

    wide = 256 if cols % 256 == 0 else LANES

    def second(q):
        for low in range(0, total, step):
            some = slice(low, low + step)

            @pl.loop(0, cols // wide)
            def _(n):
                start = pl.multiple_of(n * wide, wide)
                part = pl.ds(start, wide)
                out = dot(act[some, :], down_v[q, :, part])
                back = dot_t(dgate[some, :], gate_v[q, part, :])
                back = back + dot_t(dup[some, :], up_v[q, part, :])
                data[q, some, part] = out.astype(BF16)
                data[q, some, pl.ds(pl.multiple_of(cols + start, LANES), wide)] = back.astype(BF16)

        a_copy(q).start()

    def add(q, start, count, other):
        ref = data.at[q, pl.ds(start, count), pl.ds(0, 2 * cols)]
        ref[...] = (ref[...].astype(F32) + other.astype(F32)).astype(BF16)

    def sum_core(q):
        a_copy(q).wait_recv()
        if ny > 1:
            theirs = (ny - 1 - y) * nz * rows
            add(q, place(c, ny - 1 - y, 0), nz * rows, from_core[q, pl.ds(pl.multiple_of(theirs, rows), nz * rows), :])
            b_copy(q).start()
        add(q, place(c, y, 0), nz * rows, from_core[q, pl.ds(pl.multiple_of(y * nz * rows, rows), nz * rows), :])

    def sum_across(q):
        if ny > 1:
            b_copy(q).wait_recv()
            add(q, place(c, y, 0), nz * rows, from_y[q])
        p_sends(q, 1, lambda copy: copy.start())

    def sum_hop(q, hop):
        def arrived(way, block):
            p_copy(q, way, hop, block).wait_recv()
            if hop < nz - 1:
                add(q, place(c, y, block), rows, landing(q, way, block)[...])

        pl.when((z > 0) & (z - 1 < hop))(lambda: arrived(0, z - 1 + nz - hop))
        pl.when((z + 1 < nz) & (nz - 2 - z < hop))(lambda: arrived(1, z + 1 - nz + hop))
        if hop < nz - 1:
            p_sends(q, hop + 1, lambda copy: copy.start())
            return
        part = slice(q * 2 * cols, (q + 1) * 2 * cols)
        final[:, part] = held(q, c, y, z, 1, 2 * cols)[...].astype(F32)

        @pl.when(z > 0)
        def _():
            final[:, part] += landing(q, 0, z)[...].astype(F32)

        @pl.when(z + 1 < nz)
        def _():
            final[:, part] += landing(q, 1, z)[...].astype(F32)

    for slot in range(chunks + nz + 1):
        if slot < chunks:
            second(slot)
        for stage in range(nz + 1, 0, -1):
            q = slot - stage
            if 0 <= q < chunks:
                if stage == 1:
                    sum_core(q)
                elif stage == 2:
                    sum_across(q)
                else:
                    sum_hop(q, stage - 2)

    for q in range(chunks):
        a_copy(q).wait_send()
        if ny > 1:
            b_copy(q).wait_send()
        for hop in range(1, nz):
            p_sends(q, hop, lambda copy: copy.wait_send())

    values = tokens[...].astype(F32)
    scale = lax.rsqrt(jnp.mean(values * values, axis=-1, keepdims=True) + 1e-06)
    inner = jnp.zeros((rows, 1), F32)
    for q in range(chunks):
        part = slice(q * cols, (q + 1) * cols)
        mixed[:, part] = final[:, 2 * q * cols : (2 * q + 1) * cols].astype(BF16)
        scaled = final[:, (2 * q + 1) * cols : (2 * q + 2) * cols] * gain[:, part]
        final[:, (2 * q + 1) * cols : (2 * q + 2) * cols] = scaled
        inner = inner + jnp.sum(scaled * values[:, part], axis=-1, keepdims=True)
    inner = inner / width * scale * scale * scale
    for q in range(chunks):
        part = slice(q * cols, (q + 1) * cols)
        scaled = final[:, (2 * q + 1) * cols : (2 * q + 2) * cols]
        token_grad[:, part] = (scaled * scale - values[:, part] * inner).astype(BF16)


def local(nz, ny, tokens, norm_gain, gate_weight, up_weight, down_weight, routes, fractions, cotangent):
    rows, width = tokens.shape
    hidden = gate_weight.shape[1]
    chunks = max(1, 32 // nz)
    cols = width // chunks
    total = 2 * ny * nz * rows
    dma = pltpu.SemaphoreType.DMA
    in_vmem = pl.BlockSpec(memory_space=pltpu.VMEM)
    in_hbm = pl.BlockSpec(memory_space=pl.ANY)
    out = jax.ShapeDtypeStruct((rows, width), BF16)
    hops = max(1, nz - 1)
    return pl.pallas_call(
        functools.partial(kernel, nz, ny, chunks),
        out_shape=(out, out),
        in_specs=[in_vmem] * 5 + [in_hbm] * 3,
        out_specs=(in_vmem, in_vmem),
        scratch_shapes=[
            pltpu.VMEM((chunks, total, 2 * cols + LANES), BF16),
            pltpu.VMEM((chunks, cols, hidden), BF16),
            pltpu.VMEM((chunks, cols, hidden), BF16),
            pltpu.VMEM((chunks, hidden, cols), BF16),
            pltpu.VMEM((total, hidden), F32),
            pltpu.VMEM((total, hidden), F32),
            pltpu.VMEM((total, hidden), F32),
            pltpu.VMEM((total, hidden), BF16),
            pltpu.VMEM((total, hidden), BF16),
            pltpu.VMEM((total, hidden), BF16),
            pltpu.VMEM((chunks, total // 2, 2 * cols), BF16),
            pltpu.VMEM((chunks, nz * rows if ny > 1 else 16, 2 * cols), BF16),
            pltpu.VMEM((chunks, (nz + 1) * rows, 2 * cols), BF16),
            pltpu.VMEM((rows, 2 * width), F32),
            dma((chunks, 3)),
            dma((chunks, 2, hops)),
            dma((chunks, 2, hops)),
            dma((chunks, nz)),
            dma((chunks, nz)),
            dma((chunks, 2)),
            dma((chunks, 2)),
            dma((chunks,)),
            dma((chunks,)),
            dma((chunks,)),
            dma((chunks,)),
            dma((chunks, 2, hops)),
            dma((chunks, 2, hops)),
        ],
        compiler_params=pltpu.CompilerParams(
            collective_id=0, has_side_effects=True, vmem_limit_bytes=62 * 1024 * 1024
        ),
        cost_estimate=pl.CostEstimate(
            flops=12 * total * width * hidden,
            bytes_accessed=6 * width * hidden,
            transcendentals=total * hidden,
        ),
    )(tokens, norm_gain.reshape(1, width), routes, fractions, cotangent, gate_weight, up_weight, down_weight)


def solution(mesh):
    rows = P(("grp", "exp"), None)
    placed = (rows, P(), P(None, "exp"), P(None, "exp"), P("exp", None), rows, rows, rows)
    ny = max(1, 4 // mesh.shape["grp"])
    nz = mesh.shape["exp"] // (2 * ny)
    return jax.shard_map(
        functools.partial(local, nz, ny),
        mesh=mesh,
        in_specs=placed,
        out_specs=(rows, rows),
        check_vma=False,
    )
```

time: 240 us -> 104 us (0.43)
  Pallas kernels: 0 us -> 97.5 us
  waiting for transfers between devices: 65.2 us -> 0 us
  blocking collectives: 65 us -> 0 us
  matrix products: 54.8 us -> 0 us
  local copies, waits for them, and re-layouts: 27.1 us -> 5.85 us
  starting transfers between devices: 18.7 us -> 0 us
  other arithmetic: 7.64 us -> 0 us
    pallas_call x0 -> x1, Pallas kernels: none -> 97.5 us  [local(): pl.pallas_call(functools.partial(kernel, nz, ny, chunks), out_shape=(out,...]
    all_to_all x2 -> x0, waiting for transfers between devices: 65.2 us -> none  [the longest x1 39 us: local(): lax.all_to_all(bucket(normed_b), 'exp', split_axis=0, concat_axis=0, tile...]
    all_to_all x1 -> x0, blocking collectives: 65 us -> none  [local(): lax.all_to_all(rounded_terms, 'exp', split_axis=1, concat_axis=1, tiled=T...]
    dot_general x10 -> x0, matrix products: 54.8 us -> none  [the longest x1 9.87 us: local(): jnp.dot(dup, up_weight.T, preferred_element_type=jnp.float32)]
    all_to_all x2 -> x0, starting transfers between devices: 18.7 us -> none  [the longest x1 11.3 us: local(): lax.all_to_all(bucket(cotangent), 'exp', split_axis=0, concat_axis=0, til...]
    slice x1 -> x0, local copies, waits for them, and re-layouts: 11.3 us -> none  [local(): results[1].astype(jnp.float32)]
    another operation x5 -> x0, local copies, waits for them, and re-layouts: 10.2 us -> none  [the longest x3 7.02 us: local(): terms = jnp.stack([output.reshape(shape), backed.reshape(shape)], axis=0)]
    unnamed x21 -> x4, local copies, waits for them, and re-layouts: 0.81 us -> 5.85 us
  transfers between devices with their start and end apart: 2 -> 0, of which waited for: 2 -> 0; matrix products, arithmetic and copies ran while one was open for 7% -> 0% of each run, Pallas kernels for 0% -> 0%
where the time goes in v1:
time: 104 us
  Pallas kernels  97.5 us (94%)
  local copies, waits for them, and re-layouts  5.85 us (6%)
    pallas_call x1, Pallas kernels, local(): pl.pallas_call(functools.partial(kernel, nz, ny, chunks), out_shape=(out,...  97.5 us
    unnamed x4, local copies, waits for them, and re-layouts  5.85 us

profile of v1, /device:TPU:0, one launch (start us, length us, event | category | flops | bytes accessed | tf_op | source)
XLA Modules:
  0.0 104.0 jit_solution(357315541646564320)
XLA Ops:
  0.6 1.4 %copy.10.routes = s32[16,8]{1,0:T(8,128)} copy(s32[16,8]{0,1:T(8,128)} %param.13) | data formatting | bytes 1024 | tf_op args[5]
  2.0 1.4 %copy.11.fractions = s32[16,8]{1,0:T(8,128)} copy(s32[16,8]{0,1:T(8,128)} %param.14) | data formatting | bytes 1024 | tf_op args[6]
  3.3 97.5 %shard_map.95 = (bf16[16,4096]{1,0:T(8,128)(2,1)}, bf16[16,4096]{1,0:T(8,128)(2,1)}) custom-call(bf16[16,4096]{1,0:T(8,128)(2,1)} %tokens.1, f32[1,4096]{1,0:T(1,128)} %bitcast.1, s32[16,8]{1,0:T(8,128)} %copy.10.routes, s32[16,8]{1,0:T(8,128)} %copy.11.fractions, bf16[16,4096]{1,0:T(8,128)(2,1)} %cotangent.1, bf16[4096,1536]{1,0:T(8,128)(2,1)} %w_gate.1, ...), custom_call_target="tpu_custom_call" | custom-call | flops 19327352832 | bytes 37748736 | tf_op jit(solution)/shard_map/pallas_call | solution.py:392
  100.9 1.6 %copy.14 = bf16[16,4096]{1,0:T(8,128)(2,1)} copy(bf16[16,4096]{1,0:T(8,128)(2,1)} %get-tuple-element.4) | data formatting | bytes 262144
  102.4 1.6 %copy.15 = bf16[16,4096]{1,0:T(8,128)(2,1)} copy(bf16[16,4096]{1,0:T(8,128)(2,1)} %get-tuple-element.5) | data formatting | bytes 262144

commit v2 on v1

--- a/solution.py
+++ b/solution.py
@@ -10,6 +10,7 @@
 EXPERTS = 16
 LANES = 128
 LEAD = 2
+GAP = 2
 MESH = pl.DeviceIdType.MESH
 F32 = jnp.float32
 BF16 = jnp.bfloat16
@@ -79,9 +80,6 @@
 
     sibling = at(z, y, 1 - c)
     across = at(z, ny - 1 - y, c)
-    ahead = at(z + 1, y, c)
-    behind = at(z - 1, y, c)
-
     def weights(q):
         part = pl.ds(q * cols, cols)
         return (
@@ -98,8 +96,9 @@
     greet(sibling)
     if ny > 1:
         greet(across)
-    pl.when(z + 1 < nz)(lambda: greet(ahead))
-    pl.when(z > 0)(lambda: greet(behind))
+    peers = (2 if ny > 1 else 1) + nz - 1
+    for offset in range(1, nz):
+        greet(at(lax.rem(z + offset, nz), y, c))
 
     for q in range(chunks):
         for copy in weights(q):
@@ -120,7 +119,6 @@
         data[q, own, :cols] = normed[:, q * cols : (q + 1) * cols]
         data[q, own, cols : 2 * cols] = cotangent[:, q * cols : (q + 1) * cols]
 
-    peers = jnp.int32(2 if ny > 1 else 1) + (z + 1 < nz).astype(jnp.int32) + (z > 0).astype(jnp.int32)
     pl.semaphore_wait(barrier, peers)
 
     def span(q):
@@ -144,15 +142,15 @@
             device_id_type=MESH,
         )
 
-    def z_copy(q, way, hop, block):
+    def both(offset, visit):
+        pl.when(z + offset < nz)(lambda: visit(0, z + offset))
+        pl.when(z >= offset)(lambda: visit(1, z - offset))
+
+    def z_copy(q, way, offset, block, other):
         ref = held(q, c, y, block)
         return remote(
-            ref, ref, zs.at[q, way, hop - 1], zr.at[q, way, hop - 1], ahead if way == 0 else behind
-        )
-
-    def z_sends(q, hop, act_on):
-        pl.when((z + 1 < nz) & (z >= hop - 1))(lambda: act_on(z_copy(q, 0, hop, z - hop + 1)))
-        pl.when((z > 0) & (z + hop - 1 < nz))(lambda: act_on(z_copy(q, 1, hop, z + hop - 1)))
+            ref, ref, zs.at[q, way, offset - 1], zr.at[q, way, offset - 1], at(other, y, c)
+        )
 
     def y_copy(q, block, yy):
         ref = held(q, c, yy, block)
@@ -163,22 +161,20 @@
         return remote(ref, ref, cs.at[q, half], cr.at[q, half], sibling)
 
     def begin(q):
-        z_sends(q, 1, lambda copy: copy.start())
+        for offset in range(1, nz):
+            both(offset, lambda way, other: z_copy(q, way, offset, z, other).start())
         if ny > 1:
             y_copy(q, z, y).start()
 
-    def gather_hop(q, hop):
-        def arrived(way, block):
-            z_copy(q, way, hop, block).wait_recv()
+    def gather_z(q):
+        def arrived(way, offset, other):
+            z_copy(q, 1 - way, offset, other, other).wait_recv()
             if ny > 1:
-                y_copy(q, block, y).start()
-
-        pl.when(z >= hop)(lambda: arrived(0, z - hop))
-        pl.when(z + hop < nz)(lambda: arrived(1, z + hop))
-        if hop < nz - 1:
-            z_sends(q, hop + 1, lambda copy: copy.start())
-        else:
-            c_copy(q, c, 0).start()
+                y_copy(q, other, y).start()
+
+        for offset in range(1, nz):
+            both(offset, lambda way, other: arrived(way, offset, other))
+        c_copy(q, c, 0).start()
 
     def gather_across(q):
         if ny > 1:
@@ -216,22 +212,19 @@
 
     for q in range(min(LEAD, chunks)):
         begin(q)
-    for slot in range(chunks + nz + 1):
-        if LEAD <= slot + LEAD < chunks:
+    for slot in range(chunks + 2 * GAP + 1):
+        if slot + LEAD < chunks:
             begin(slot + LEAD)
-        for stage in range(nz, 0, -1):
-            q = slot - stage + 1
-            if 0 <= q < chunks:
-                if stage < nz:
-                    gather_hop(q, stage)
-                else:
-                    gather_across(q)
-        if 0 <= slot - nz < chunks:
-            first(slot - nz)
-
-    for q in range(chunks):
-        for hop in range(1, nz):
-            z_sends(q, hop, lambda copy: copy.wait_send())
+        if 0 <= slot - GAP < chunks:
+            gather_across(slot - GAP)
+        if slot < chunks:
+            gather_z(slot)
+        if 0 <= slot - 2 * GAP < chunks:
+            first(slot - 2 * GAP)
+
+    for q in range(chunks):
+        for offset in range(1, nz):
+            both(offset, lambda way, other: z_copy(q, way, offset, z, other).wait_send())
         if ny > 1:
             for block in range(nz):
                 y_copy(q, block, y).wait_send()
@@ -268,21 +261,17 @@
             held(q, c, ny - 1 - y, 0, nz, 2 * cols), from_y.at[q], b_s.at[q], b_r.at[q], across
         )
 
-    def landing(q, way, block):
-        return from_z.at[q, pl.ds(pl.multiple_of((block + 1 - way) * rows, rows), rows), :]
-
-    def p_copy(q, way, hop, block):
+    def landing(q, source):
+        return from_z.at[q, pl.ds(pl.multiple_of(source * rows, rows), rows), :]
+
+    def p_copy(q, way, offset, block, source):
         return remote(
             held(q, c, y, block, 1, 2 * cols),
-            landing(q, way, block),
-            ps.at[q, way, hop - 1],
-            pr.at[q, way, hop - 1],
-            ahead if way == 0 else behind,
-        )
-
-    def p_sends(q, hop, act_on):
-        pl.when(z < hop)(lambda: act_on(p_copy(q, 0, hop, z + nz - hop)))
-        pl.when(nz - 1 - z < hop)(lambda: act_on(p_copy(q, 1, hop, z - nz + hop)))
+            landing(q, source),
+            ps.at[q, way, offset - 1],
+            pr.at[q, way, offset - 1],
+            at(block, y, c),
+        )
 
     wide = 256 if cols % 256 == 0 else LANES
 
@@ -318,49 +307,36 @@
         if ny > 1:
             b_copy(q).wait_recv()
             add(q, place(c, y, 0), nz * rows, from_y[q])
-        p_sends(q, 1, lambda copy: copy.start())
-
-    def sum_hop(q, hop):
-        def arrived(way, block):
-            p_copy(q, way, hop, block).wait_recv()
-            if hop < nz - 1:
-                add(q, place(c, y, block), rows, landing(q, way, block)[...])
-
-        pl.when((z > 0) & (z - 1 < hop))(lambda: arrived(0, z - 1 + nz - hop))
-        pl.when((z + 1 < nz) & (nz - 2 - z < hop))(lambda: arrived(1, z + 1 - nz + hop))
-        if hop < nz - 1:
-            p_sends(q, hop + 1, lambda copy: copy.start())
-            return
+        for offset in range(1, nz):
+            both(offset, lambda way, other: p_copy(q, way, offset, other, z).start())
+
+    def sum_z(q):
         part = slice(q * 2 * cols, (q + 1) * 2 * cols)
         final[:, part] = held(q, c, y, z, 1, 2 * cols)[...].astype(F32)
 
-        @pl.when(z > 0)
-        def _():
-            final[:, part] += landing(q, 0, z)[...].astype(F32)
-
-        @pl.when(z + 1 < nz)
-        def _():
-            final[:, part] += landing(q, 1, z)[...].astype(F32)
-
-    for slot in range(chunks + nz + 1):
+        def arrived(way, offset, other):
+            p_copy(q, 1 - way, offset, other, other).wait_recv()
+            final[:, part] += landing(q, other)[...].astype(F32)
+
+        for offset in range(1, nz):
+            both(offset, lambda way, other: arrived(way, offset, other))
+
+    for slot in range(chunks + 3 * GAP):
         if slot < chunks:
             second(slot)
-        for stage in range(nz + 1, 0, -1):
-            q = slot - stage
-            if 0 <= q < chunks:
-                if stage == 1:
-                    sum_core(q)
-                elif stage == 2:
-                    sum_across(q)
-                else:
-                    sum_hop(q, stage - 2)
+        if 0 <= slot - 3 * GAP < chunks:
+            sum_z(slot - 3 * GAP)
+        if 0 <= slot - 2 * GAP < chunks:
+            sum_across(slot - 2 * GAP)
+        if 0 <= slot - GAP < chunks:
+            sum_core(slot - GAP)
 
     for q in range(chunks):
         a_copy(q).wait_send()
         if ny > 1:
             b_copy(q).wait_send()
-        for hop in range(1, nz):
-            p_sends(q, hop, lambda copy: copy.wait_send())
+        for offset in range(1, nz):
+            both(offset, lambda way, other: p_copy(q, way, offset, other, z).wait_send())
 
     values = tokens[...].astype(F32)
     scale = lax.rsqrt(jnp.mean(values * values, axis=-1, keepdims=True) + 1e-06)
@@ -407,7 +383,7 @@
             pltpu.VMEM((total, hidden), BF16),
             pltpu.VMEM((chunks, total // 2, 2 * cols), BF16),
             pltpu.VMEM((chunks, nz * rows if ny > 1 else 16, 2 * cols), BF16),
-            pltpu.VMEM((chunks, (nz + 1) * rows, 2 * cols), BF16),
+            pltpu.VMEM((chunks, nz * rows, 2 * cols), BF16),
             pltpu.VMEM((rows, 2 * width), F32),
             dma((chunks, 3)),
             dma((chunks, 2, hops)),

time: 104 us -> 90.1 us (0.87)
  Pallas kernels: 97.5 us -> 83.3 us
    pallas_call x1, Pallas kernels: 97.5 us -> 83.3 us  [local(): pl.pallas_call(functools.partial(kernel, nz, ny, chunks), out_shape=(out,...]
where the time goes in v2:
time: 90.1 us; the launch traced here: 89.8 us
  Pallas kernels  83.3 us (92%)
  local copies, waits for them, and re-layouts  5.85 us (6%)
    pallas_call x1, Pallas kernels, local(): pl.pallas_call(functools.partial(kernel, nz, ny, chunks), out_shape=(out,...  83.3 us
    unnamed x4, local copies, waits for them, and re-layouts  5.85 us

profile of v2, /device:TPU:0, one launch (start us, length us, event | category | flops | bytes accessed | tf_op | source)
XLA Modules:
  0.0 89.8 jit_solution(7382155285815587641)
XLA Ops:
  0.6 1.4 %copy.10.routes = s32[16,8]{1,0:T(8,128)} copy(s32[16,8]{0,1:T(8,128)} %param.13) | data formatting | bytes 1024 | tf_op args[5]
  2.0 1.4 %copy.11.fractions = s32[16,8]{1,0:T(8,128)} copy(s32[16,8]{0,1:T(8,128)} %param.14) | data formatting | bytes 1024 | tf_op args[6]
  3.3 83.3 %shard_map.95 = (bf16[16,4096]{1,0:T(8,128)(2,1)}, bf16[16,4096]{1,0:T(8,128)(2,1)}) custom-call(bf16[16,4096]{1,0:T(8,128)(2,1)} %tokens.1, f32[1,4096]{1,0:T(1,128)} %bitcast.1, s32[16,8]{1,0:T(8,128)} %copy.10.routes, s32[16,8]{1,0:T(8,128)} %copy.11.fractions, bf16[16,4096]{1,0:T(8,128)(2,1)} %cotangent.1, bf16[4096,1536]{1,0:T(8,128)(2,1)} %w_gate.1, ...), custom_call_target="tpu_custom_call" | custom-call | flops 19327352832 | bytes 37748736 | tf_op jit(solution)/shard_map/pallas_call | solution.py:368
  86.7 1.6 %copy.14 = bf16[16,4096]{1,0:T(8,128)(2,1)} copy(bf16[16,4096]{1,0:T(8,128)(2,1)} %get-tuple-element.4) | data formatting | bytes 262144
  88.3 1.6 %copy.15 = bf16[16,4096]{1,0:T(8,128)(2,1)} copy(bf16[16,4096]{1,0:T(8,128)(2,1)} %get-tuple-element.5) | data formatting | bytes 262144
